TPU v7x, 256 devices: a whole 4x4x8 slice. The times are simulated.
256 devices in a mesh: freq: 2 (over core), ma: 128 (over z, x, y).
Axes of the slice: x: 4, y: 4, z: 8, core: 2. Of those that a mesh axis runs over, the one named last changes fastest.
Arguments:
- visibility: float32 [4, 2048, 16384], P('freq', 'ma'), parts along dimension 0, may hold values from -6 to 6
- slot_mode: int32 [128], replicated, may hold values from 0 to 127, as said below
- mode_rank: int32 [128], replicated, may hold values from 8 to 64
- beam_svd: bfloat16 [256, 64, 65536], P(('freq', 'ma')), parts along dimension 0, may hold values from -0.0234375 to 0.0234375
- signal_eigen: float32 [256, 64], P(('freq', 'ma')), parts along dimension 0, may hold values from 0.1 to 10
- sky_map: bfloat16 [256, 64, 2402], P(('freq', 'ma')), parts along dimension 0, may hold values from -0.75 to 0.75
Outputs:
- alm: float32 [256, 2402], P(('freq', 'ma')), parts along dimension 0
There are 2 independent parts, one for each index of `freq`. A program takes and returns all parts, laid end to end along the dimension named above; an argument that names none is the same for every part. Nothing has to cross between parts.
Inputs may be any that keep to these rules, and one draw needn't show every extreme that they name: `slot_mode`: a permutation of 0 to 127.
All inputs are finite; a program needn't handle non-finite values.
Results may differ from a plain program's by a relative error of at most 0.006.
Values may be sent and summed in bfloat16 or wider, within the bound.
A program may use at most 128 MiB of HBM per device.

v0:
```python
import functools
import math

import jax
import jax.numpy as jnp
from jax import lax
from jax.experimental import pallas as pl
from jax.experimental.pallas import tpu as pltpu
from jax.sharding import PartitionSpec as P

MESH = pl.DeviceIdType.MESH
NZ, NX, NY = 8, 4, 4
NP = NX * NY
NSUB = 8
GSUB = 4
NG = NSUB // GSUB
W = 128
F32, BF16 = jnp.float32, jnp.bfloat16

CHAIN = {4: 3, 3: 2, 2: 1, 1: 0}
THREE = {4: 3, 3: 1, 2: 1, 1: 0}
TREE = {4: 2, 3: 2, 2: 0, 1: 0}
DIRECT = {4: 0, 3: 0, 2: 0, 1: 0}
AHEAD = 4
PLANS = (TREE,) * 7 + (DIRECT,)
LEVELS = 5
NODES = ((1, 3), (-1, 3), (0, 4), (1, 2), (-1, 2), (1, 1), (-1, 1))


def z_plan(s):
    sign4 = 1 if s % 2 == 0 else -1
    parent = PLANS[s]
    nodes = [(side or sign4, d, slot) for slot, (side, d) in enumerate(NODES)]

    def children(sign, d):
        return [n for n in nodes if d and n[0] == sign and parent[n[1]] == d]

    def level(sign, d):
        below = [n for n in nodes if parent[n[1]] == 0] if d == 0 else children(sign, d)
        return max((1 + level(n[0], n[1]) for n in below), default=0)

    last = level(0, 0)
    sends = [[] for _ in range(last)]
    counts = [0] * (last + 1)
    for sign, d, slot in nodes:
        to = parent[d]
        to_level = level(sign if to else 0, to)
        counts[to_level] += 1
        sends[level(sign, d)].append((slot, sign, d, to, to_level, [n[2] for n in children(sign, d)]))
    for group in sends:
        group.sort(key=lambda n: -n[2])
    arrivals = [n[2] for n in nodes if parent[n[1]] == 0]
    return last, sends, counts, arrivals


def schedule():
    events = []
    for s in range(NSUB):
        last, sends, _, _ = z_plan(s)
        ready = [S_FIRST + S_EACH * s] + [0.0] * last
        for k in range(last + 1):
            events.append((ready[k], s, k))
            for _, _, d, to, to_level, _ in (sends[k] if k < last else ()):
                ready[to_level] = max(ready[to_level], ready[k] + HOP + LINK * (d - to))
    return [(s, k) for _, s, k in sorted(events)]


S_FIRST, S_EACH, HOP, LINK = 5.0, 1.43, 4.0, 0.8


def sin_cos(index, period):
    quarter = period // 4
    shifted = index + quarter // 2
    quadrant = (shifted // quarter) % 4
    small = (shifted % quarter) - quarter // 2
    a = small.astype(F32) * F32(2.0 * math.pi / period)
    a2 = a * a
    s = a * (1.0 + a2 * (-1.0 / 6 + a2 * (1.0 / 120 + a2 * (-1.0 / 5040 + a2 * (1.0 / 362880)))))
    c = 1.0 + a2 * (-0.5 + a2 * (1.0 / 24 + a2 * (-1.0 / 720 + a2 * (1.0 / 40320))))
    odd = (quadrant % 2) == 1
    sin = jnp.where(odd, c, s)
    cos = jnp.where(odd, s, c)
    sin = jnp.where(quadrant >= 2, -sin, sin)
    cos = jnp.where((quadrant == 1) | (quadrant == 2), -cos, cos)
    return sin, cos


def column_of(row, n):
    r = lax.broadcasted_iota(jnp.int32, (n, n), 0)
    c = lax.broadcasted_iota(jnp.int32, (n, n), 1)
    return jnp.sum(jnp.where(r == c, jnp.broadcast_to(row, (n, n)), 0.0), axis=1, keepdims=True)


def kernel(
    vis, slot, rank, beam, eigen, sky, out,
    vis_v, slot_v, rank_v, beam_v, eigen_v, sky_v,
    vb, xs, tab, part, zbuf, bbuf, fsum, ob, modes,
    vis_sem, small_sem, beam_sem, sky_sem,
    s1_send, s1_recv, z_send, z_recv, s3_send, s3_recv,
):
    i = lax.axis_index("ma")
    z, p = i // NP, i % NP
    x, y = p // NY, p % NY
    modes_total = slot.shape[1]
    times = vis.shape[1]
    total = times * NZ * NP
    plane_times = times * NP

    def plane(dx, dy):
        return ((x + dx) % NX) * NY + (y + dy) % NY

    def zdev(d):
        return {"ma": ((z + d + NZ) % NZ) * NP + p}

    offsets = sorted(
        ((dx, dy) for dx in range(NX) for dy in range(NY) if (dx, dy) != (0, 0)),
        key=lambda o: -min(o[0], NX - o[0]) - min(o[1], NY - o[1]),
    )
    hops = {sign * (d - to) for s in range(NSUB) for group in z_plan(s)[1] for _, sign, d, to, _, _ in group}
    zoffs = sorted({h % NZ for h in hops} | {-h % NZ for h in hops})

    pieces = vis_sem.shape[0]
    span = vis.shape[2] // pieces
    for q in range(pieces):
        cols = pl.ds(q * span, span)
        pltpu.make_async_copy(vis.at[:, :, cols], vis_v.at[:, :, cols], vis_sem.at[q]).start()
    small = [(slot, slot_v), (rank, rank_v), (eigen, eigen_v)]
    for n, (src, dst) in enumerate(small):
        pltpu.make_async_copy(src, dst, small_sem.at[n]).start()

    barrier = pltpu.get_barrier_semaphore()
    for dx, dy in offsets:
        pl.semaphore_signal(barrier, 1, device_id={"ma": z * NP + plane(dx, dy)}, device_id_type=MESH)
    for d in zoffs:
        pl.semaphore_signal(barrier, 1, device_id=zdev(d), device_id_type=MESH)

    for q in range(pieces):
        cols = pl.ds(q * span, span)
        pltpu.make_async_copy(vis.at[:, :, cols], vis_v.at[:, :, cols], vis_sem.at[q]).wait()

        def cast(b, carry):
            for s in range(NSUB):
                for c in range(2):
                    at = pl.multiple_of(b * (NSUB * W) + s * W, W)
                    vb[s, b, :, c * W:(c + 1) * W] = vis_v[c, :, pl.ds(at, W)].astype(BF16)
            return carry

        per = NP // pieces
        lax.fori_loop(q * per, (q + 1) * per, cast, 0)
    pltpu.make_async_copy(beam.at[0], beam_v, beam_sem).start()
    pltpu.make_async_copy(sky.at[0], sky_v, sky_sem).start()

    pl.semaphore_wait(barrier, len(offsets) + len(zoffs))
    def send_sub(s, carry):
        for dx, dy in offsets:
            to = plane(dx, dy)
            pltpu.make_async_remote_copy(
                src_ref=vb.at[s, to], dst_ref=xs.at[s, p], send_sem=s1_send.at[s], recv_sem=s1_recv.at[s],
                device_id={"ma": z * NP + to}, device_id_type=MESH,
            ).start()
        return carry

    lax.fori_loop(0, AHEAD, send_sub, 0)

    for s in range(NSUB):
        xs[s, p] = vb[s, p]
    for n, (src, dst) in enumerate(small):
        pltpu.make_async_copy(src, dst, small_sem.at[n]).wait()
    slot_f = slot_v[...].astype(F32)
    wave = (column_of(slot_f, modes_total) + 1.0).astype(jnp.int32)
    t = z * plane_times + lax.broadcasted_iota(jnp.int32, (modes_total, plane_times), 1)
    sin, cos = sin_cos((wave * t) % total, total)
    scale = F32(1.0 / math.sqrt(total))
    for n, table in enumerate((cos * scale, sin * scale)):
        high = table.astype(BF16)
        rows = pl.ds(n * modes_total, modes_total)
        tab[0, rows, :] = high
        tab[1, rows, :] = (table - high.astype(F32)).astype(BF16)
    lanes = lax.broadcasted_iota(jnp.int32, (1, modes_total), 1)
    own_mode = jnp.sum(jnp.where(lanes == i, slot_f, 0.0), axis=1, keepdims=True)
    own_rank = jnp.sum(
        jnp.where(lanes.astype(F32) == own_mode, rank_v[...].astype(F32), 0.0), axis=1, keepdims=True
    )
    levels = eigen_v.shape[1]
    eig = column_of(eigen_v[...], levels)
    level = lax.broadcasted_iota(jnp.int32, (levels, 1), 0).astype(F32)
    weight = jnp.where(level < own_rank, eig / (1.0 + eig), 0.0)

    def zrow(d):
        return (z + d + NZ) % NZ

    def transform(s):
        blocks = pl.ds(0, NP - 1)
        pltpu.make_async_copy(xs.at[s, blocks], xs.at[s, blocks], s1_recv.at[s]).wait()
        if s + AHEAD < NSUB:
            send_sub(s + AHEAD, 0)
        block = xs[s].reshape(plane_times, 2 * W)
        res = jnp.dot(tab[0], block, preferred_element_type=F32) + jnp.dot(
            tab[1], block, preferred_element_type=F32
        )
        m = modes_total
        cr, ci, sr, si = res[:m, :W], res[:m, W:], res[m:, :W], res[m:, W:]
        for n, v in enumerate((cr + si, ci - sr, cr - si, ci + sr)):
            part[s, :, n] = v.astype(BF16).reshape(NZ, NP, W)

    def z_step(s, k):
        last, sends, counts, arrivals = z_plan(s)
        if k == 0:
            transform(s)
        else:
            some = pl.ds(0, counts[k])
            pltpu.make_async_copy(zbuf.at[s, some], zbuf.at[s, some], z_recv.at[s, k]).wait()
        if k == last:
            v = part[s, z].astype(F32)
            for slot in arrivals:
                v = v + zbuf[s, slot].astype(F32)
            for n in range(4):
                fsum[s // GSUB, :, (s % GSUB) * 4 + n, :] = v[n]
            return
        for slot, sign, d, to, to_level, below in sends[k]:
            src = part.at[s, zrow(sign * d)]
            if below:
                v = src[...].astype(F32)
                for c in below:
                    v = v + zbuf[s, c].astype(F32)
                src = bbuf.at[s, slot]
                src[...] = v.astype(BF16)
            pltpu.make_async_remote_copy(
                src_ref=src, dst_ref=zbuf.at[s, slot], send_sem=z_send.at[s], recv_sem=z_recv.at[s, to_level],
                device_id=zdev(sign * (d - to)), device_id_type=MESH,
            ).start()

    def exchange(g):
        ob[g] = fsum[g].astype(BF16)
        for n, (dx, dy) in enumerate(offsets):
            to = plane(dx, dy)
            pltpu.make_async_remote_copy(
                src_ref=ob.at[g, to], dst_ref=modes.at[g, p], send_sem=s3_send.at[g],
                recv_sem=s3_recv.at[g, n], device_id={"ma": z * NP + to}, device_id_type=MESH,
            ).start()

    baselines = vis.shape[2]

    def project_one(b, rows, g, acc):
        for s in range(GSUB):
            for n in range(4):
                at = pl.multiple_of(n * baselines + b * (NSUB * W) + (g * GSUB + s) * W, W)
                r = s * 4 + n
                acc = acc + beam_v[:, pl.ds(at, W)].astype(F32) * rows[r:r + 1, :]
        return acc

    def project(g, acc):
        acc = project_one(p, ob[g, p].astype(F32), g, acc)
        for n in reversed(range(len(offsets))):
            dx, dy = offsets[n]
            b = plane(NX - dx, NY - dy)
            pltpu.make_async_copy(modes.at[g, b], modes.at[g, b], s3_recv.at[g, n]).wait()
            acc = project_one(b, modes[g, b].astype(F32), g, acc)
        return acc

    done = [0] * NG
    for s, k in schedule():
        z_step(s, k)
        if k == z_plan(s)[0]:
            g = s // GSUB
            done[g] += 1
            if done[g] == GSUB:
                exchange(g)
    pltpu.make_async_copy(beam.at[0], beam_v, beam_sem).wait()
    pltpu.make_async_copy(sky.at[0], sky_v, sky_sem).wait()
    acc = jnp.zeros((levels, W), F32)
    for g in range(NG):
        acc = project(g, acc)
    filtered = jnp.sum(acc, axis=1, keepdims=True) * weight
    out[...] = jnp.sum(sky_v[...].astype(F32) * filtered, axis=0, keepdims=True)

    for s in range(NSUB):
        blocks = pl.ds(0, NP - 1)
        pltpu.make_async_copy(vb.at[s, blocks], vb.at[s, blocks], s1_send.at[s]).wait()
        pltpu.make_async_copy(zbuf.at[s], zbuf.at[s], z_send.at[s]).wait()
    for g in range(NG):
        blocks = pl.ds(0, NP - 1)
        pltpu.make_async_copy(ob.at[g, blocks], ob.at[g, blocks], s3_send.at[g]).wait()


def per_device(visibility, slot_mode, mode_rank, beam_svd, signal_eigen, sky_map):
    count = slot_mode.shape[0]
    levels, entries = beam_svd.shape[1:]
    multipoles = sky_map.shape[2]
    times = visibility.shape[1]
    any_spec = pl.BlockSpec(memory_space=pl.ANY)
    dma = pltpu.SemaphoreType.DMA
    return pl.pallas_call(
        kernel,
        out_shape=jax.ShapeDtypeStruct((1, multipoles), F32),
        in_specs=[any_spec] * 6,
        out_specs=pl.BlockSpec(memory_space=pltpu.VMEM),
        scratch_shapes=[
            pltpu.VMEM(visibility.shape, F32),
            pltpu.VMEM((1, count), jnp.int32),
            pltpu.VMEM((1, count), jnp.int32),
            pltpu.VMEM((levels, entries), BF16),
            pltpu.VMEM((1, levels), F32),
            pltpu.VMEM((levels, multipoles), BF16),
            pltpu.VMEM((NSUB, NP, times, 2 * W), BF16),
            pltpu.VMEM((NSUB, NP, times, 2 * W), BF16),
            pltpu.VMEM((2, 2 * count, times * NP), BF16),
            pltpu.VMEM((NSUB, NZ, 4, NP, W), BF16),
            pltpu.VMEM((NSUB, 7, 4, NP, W), BF16),
            pltpu.VMEM((NSUB, 7, 4, NP, W), BF16),
            pltpu.VMEM((NG, NP, 4 * GSUB, W), F32),
            pltpu.VMEM((NG, NP, 4 * GSUB, W), BF16),
            pltpu.VMEM((NG, NP, 4 * GSUB, W), BF16),
            dma((4,)), dma((3,)), dma, dma,
            dma((NSUB,)), dma((NSUB,)), dma((NSUB,)), dma((NSUB, LEVELS)), dma((NG,)), dma((NG, NP - 1)),
        ],
        compiler_params=pltpu.CompilerParams(
            collective_id=0, has_side_effects=True, vmem_limit_bytes=60 * 2**20
        ),
    )(
        visibility, slot_mode.reshape(1, count), mode_rank.reshape(1, count), beam_svd, signal_eigen, sky_map
    )


def solution(mesh):
    return jax.shard_map(
        per_device,
        mesh=mesh,
        in_specs=(
            P("freq", "ma", None),
            P(),
            P(),
            P(("freq", "ma"), None, None),
            P(("freq", "ma"), None),
            P(("freq", "ma"), None, None),
        ),
        out_specs=P(("freq", "ma"), None),
        check_vma=False,
    )
```

profile of v0, /device:TPU:2, one launch (start us, length us, event | category | flops | bytes accessed | tf_op | source)
XLA Modules:
  0.0 40.6 jit_solution(12359128615160243936)
XLA Ops:
  0.0 39.3 %shard_map.64 = f32[1,2402]{1,0:T(1,128)} custom-call(f32[2,16,16384]{2,1,0:T(8,128)} %vis.1, s32[1,128]{1,0:T(1,128)} %bitcast.2, s32[1,128]{1,0:T(1,128)} %bitcast.3, bf16[1,64,65536]{2,1,0:T(8,128)(2,1)} %beam.1, f32[1,64]{1,0:T(1,128)} %eigen.1, bf16[1,64,2402]{2,1,0:T(8,128)(2,1)} %sky.1), custom_call_target="tpu_custom_call" | custom-call | tf_op jit(solution)/shard_map/pallas_call | solution.py:293
  39.3 1.3 %copy.8 = f32[1,2402]{1,0:T(1,128)} copy(f32[1,2402]{1,0:T(1,128)} %shard_map.64) | data formatting | bytes 19216
where the time goes:
time: 41 us; the launch traced here: 40.6 us
  Pallas kernels  39.3 us (96%)
  local copies, waits for them, and re-layouts  1.3 us (3%)
    pallas_call x1, Pallas kernels, per_device(): pl.pallas_call(kernel, out_shape=jax.ShapeDtypeStruct((1, multipoles), F3...  39.3 us
    unnamed x1, local copies, waits for them, and re-layouts  1.3 us

commit v1 on v0

--- a/solution.py
+++ b/solution.py
@@ -21,9 +21,11 @@
 THREE = {4: 3, 3: 1, 2: 1, 1: 0}
 TREE = {4: 2, 3: 2, 2: 0, 1: 0}
 DIRECT = {4: 0, 3: 0, 2: 0, 1: 0}
-AHEAD = 4
-PLANS = (TREE,) * 7 + (DIRECT,)
+SINGLES = 4
+PAIRS = (NSUB - SINGLES) // 2
+PLANS = (TREE,) * SINGLES
 LEVELS = 5
+PAIR_HOPS = (4, 3, -3, 2, -2, 1, -1)
 NODES = ((1, 3), (-1, 3), (0, 4), (1, 2), (-1, 2), (1, 1), (-1, 1))
 
 
@@ -55,17 +57,16 @@
 
 def schedule():
     events = []
-    for s in range(NSUB):
-        last, sends, _, _ = z_plan(s)
-        ready = [S_FIRST + S_EACH * s] + [0.0] * last
-        for k in range(last + 1):
-            events.append((ready[k], s, k))
-            for _, _, d, to, to_level, _ in (sends[k] if k < last else ()):
-                ready[to_level] = max(ready[to_level], ready[k] + HOP + LINK * (d - to))
-    return [(s, k) for _, s, k in sorted(events)]
-
-
-S_FIRST, S_EACH, HOP, LINK = 5.0, 1.43, 4.0, 0.8
+    for s in range(SINGLES):
+        for k in range(z_plan(s)[0] + 1):
+            events.append((S_EACH * s + (FIRST + LATER * (k - 1) if k else 0.0), s, k))
+    for g in range(PAIRS):
+        t = S_EACH * (SINGLES + 1 + 2 * g)
+        events += [(t, g, "start"), (t + PAIR_COPY, g, "end")]
+    return [(s, k) for _, s, k in sorted(events, key=lambda e: e[0])]
+
+
+S_EACH, FIRST, LATER, PAIR_COPY = 1.43, 4.2, 4.6, 8.0
 
 
 def sin_cos(index, period):
@@ -97,6 +98,7 @@
     vb, xs, tab, part, zbuf, bbuf, fsum, ob, modes,
     vis_sem, small_sem, beam_sem, sky_sem,
     s1_send, s1_recv, z_send, z_recv, s3_send, s3_recv,
+    pv, xp, zp, pair_send, pair_recv, s1p_send, s1p_recv, zp_send, zp_recv,
 ):
     i = lax.axis_index("ma")
     z, p = i // NP, i % NP
@@ -116,7 +118,8 @@
         ((dx, dy) for dx in range(NX) for dy in range(NY) if (dx, dy) != (0, 0)),
         key=lambda o: -min(o[0], NX - o[0]) - min(o[1], NY - o[1]),
     )
-    hops = {sign * (d - to) for s in range(NSUB) for group in z_plan(s)[1] for _, sign, d, to, _, _ in group}
+    hops = {sign * (d - to) for s in range(SINGLES) for group in z_plan(s)[1] for _, sign, d, to, _, _ in group}
+    hops |= set(range(1, NZ)) if PAIRS else set()
     zoffs = sorted({h % NZ for h in hops} | {-h % NZ for h in hops})
 
     pieces = vis_sem.shape[0]
@@ -128,6 +131,9 @@
     for n, (src, dst) in enumerate(small):
         pltpu.make_async_copy(src, dst, small_sem.at[n]).start()
 
+    def zrow(d):
+        return (z + d + NZ) % NZ
+
     barrier = pltpu.get_barrier_semaphore()
     for dx, dy in offsets:
         pl.semaphore_signal(barrier, 1, device_id={"ma": z * NP + plane(dx, dy)}, device_id_type=MESH)
@@ -151,31 +157,54 @@
     pltpu.make_async_copy(sky.at[0], sky_v, sky_sem).start()
 
     pl.semaphore_wait(barrier, len(offsets) + len(zoffs))
-    def send_sub(s, carry):
+    upper = [(z + g) % 2 for g in range(PAIRS)]
+    kept = [SINGLES + 2 * g + upper[g] for g in range(PAIRS)]
+    given = [SINGLES + 2 * g + 1 - upper[g] for g in range(PAIRS)]
+    other = [1 - 2 * upper[g] for g in range(PAIRS)]
+
+    for g in range(PAIRS):
+        pltpu.make_async_remote_copy(
+            src_ref=vb.at[given[g]], dst_ref=pv.at[g], send_sem=pair_send.at[g], recv_sem=pair_recv.at[g],
+            device_id=zdev(other[g]), device_id_type=MESH,
+        ).start()
+
+    def send_blocks(src, dst, send_sem, recv_sem):
         for dx, dy in offsets:
             to = plane(dx, dy)
             pltpu.make_async_remote_copy(
-                src_ref=vb.at[s, to], dst_ref=xs.at[s, p], send_sem=s1_send.at[s], recv_sem=s1_recv.at[s],
+                src_ref=src.at[to], dst_ref=dst.at[p], send_sem=send_sem, recv_sem=recv_sem,
                 device_id={"ma": z * NP + to}, device_id_type=MESH,
             ).start()
+
+    def send_single(s, carry):
+        send_blocks(vb.at[s], xs.at[s], s1_send.at[s], s1_recv.at[s])
         return carry
 
-    lax.fori_loop(0, AHEAD, send_sub, 0)
-
-    for s in range(NSUB):
+    lax.fori_loop(0, SINGLES, send_single, 0)
+    for g in range(PAIRS):
+        send_blocks(vb.at[kept[g]], xp.at[g, 0], s1p_send.at[g], s1p_recv.at[g])
+
+    for s in range(SINGLES):
         xs[s, p] = vb[s, p]
+    for g in range(PAIRS):
+        xp[g, 0, p] = vb[kept[g], p]
     for n, (src, dst) in enumerate(small):
         pltpu.make_async_copy(src, dst, small_sem.at[n]).wait()
     slot_f = slot_v[...].astype(F32)
     wave = (column_of(slot_f, modes_total) + 1.0).astype(jnp.int32)
-    t = z * plane_times + lax.broadcasted_iota(jnp.int32, (modes_total, plane_times), 1)
-    sin, cos = sin_cos((wave * t) % total, total)
     scale = F32(1.0 / math.sqrt(total))
-    for n, table in enumerate((cos * scale, sin * scale)):
-        high = table.astype(BF16)
-        rows = pl.ds(n * modes_total, modes_total)
-        tab[0, rows, :] = high
-        tab[1, rows, :] = (table - high.astype(F32)).astype(BF16)
+    for q, d in enumerate([0] + other):
+        t = zrow(d) * plane_times + lax.broadcasted_iota(jnp.int32, (modes_total, plane_times), 1)
+        sin, cos = sin_cos((wave * t) % total, total)
+        for n, table in enumerate((cos * scale, sin * scale)):
+            high = table.astype(BF16)
+            rows = pl.ds(n * modes_total, modes_total)
+            tab[q, 0, rows, :] = high
+            tab[q, 1, rows, :] = (table - high.astype(F32)).astype(BF16)
+    for g in range(PAIRS):
+        pltpu.make_async_copy(pv.at[g], pv.at[g], pair_recv.at[g]).wait()
+        send_blocks(pv.at[g], xp.at[g, 1], s1p_send.at[g], s1p_recv.at[g])
+        xp[g, 1, p] = pv[g, p]
     lanes = lax.broadcasted_iota(jnp.int32, (1, modes_total), 1)
     own_mode = jnp.sum(jnp.where(lanes == i, slot_f, 0.0), axis=1, keepdims=True)
     own_rank = jnp.sum(
@@ -186,22 +215,51 @@
     level = lax.broadcasted_iota(jnp.int32, (levels, 1), 0).astype(F32)
     weight = jnp.where(level < own_rank, eig / (1.0 + eig), 0.0)
 
-    def zrow(d):
-        return (z + d + NZ) % NZ
-
-    def transform(s):
-        blocks = pl.ds(0, NP - 1)
-        pltpu.make_async_copy(xs.at[s, blocks], xs.at[s, blocks], s1_recv.at[s]).wait()
-        if s + AHEAD < NSUB:
-            send_sub(s + AHEAD, 0)
-        block = xs[s].reshape(plane_times, 2 * W)
-        res = jnp.dot(tab[0], block, preferred_element_type=F32) + jnp.dot(
-            tab[1], block, preferred_element_type=F32
+    def partial_modes(block, q):
+        return jnp.dot(tab[q, 0], block, preferred_element_type=F32) + jnp.dot(
+            tab[q, 1], block, preferred_element_type=F32
         )
+
+    def store_parts(s, res):
         m = modes_total
         cr, ci, sr, si = res[:m, :W], res[:m, W:], res[m:, :W], res[m:, W:]
         for n, v in enumerate((cr + si, ci - sr, cr - si, ci + sr)):
             part[s, :, n] = v.astype(BF16).reshape(NZ, NP, W)
+
+    def transform(s):
+        blocks = pl.ds(0, NP - 1)
+        pltpu.make_async_copy(xs.at[s, blocks], xs.at[s, blocks], s1_recv.at[s]).wait()
+        store_parts(s, partial_modes(xs[s].reshape(plane_times, 2 * W), 0))
+
+    def pair_start(g):
+        blocks = pl.ds(0, NP - 1)
+        pltpu.make_async_copy(xp.at[g, :, blocks], xp.at[g, :, blocks], s1p_recv.at[g]).wait()
+        store_parts(
+            SINGLES + g,
+            partial_modes(xp[g, 0].reshape(plane_times, 2 * W), 0)
+            + partial_modes(xp[g, 1].reshape(plane_times, 2 * W), 1 + g),
+        )
+        for n, d in enumerate(PAIR_HOPS):
+            pltpu.make_async_remote_copy(
+                src_ref=part.at[SINGLES + g, zrow(d)], dst_ref=zp.at[g, n], send_sem=zp_send.at[g],
+                recv_sem=zp_recv.at[g], device_id=zdev(d), device_id_type=MESH,
+            ).start()
+
+    def pair_end(g):
+        pltpu.make_async_copy(zp.at[g], zp.at[g], zp_recv.at[g]).wait()
+        mine = part[SINGLES + g, z].astype(F32)
+        others = jnp.zeros_like(mine)
+        for n, d in enumerate(PAIR_HOPS):
+            if d % 2 == 0:
+                mine = mine + zp[g, n].astype(F32)
+            else:
+                others = others + zp[g, n].astype(F32)
+        first = jnp.where(upper[g] == 0, mine, others)
+        second = jnp.where(upper[g] == 0, others, mine)
+        for m, v in enumerate((first, second)):
+            s = SINGLES + 2 * g + m
+            for n in range(4):
+                fsum[s // GSUB, :, (s % GSUB) * 4 + n, :] = v[n]
 
     def z_step(s, k):
         last, sends, counts, arrivals = z_plan(s)
@@ -260,9 +318,17 @@
 
     done = [0] * NG
     for s, k in schedule():
-        z_step(s, k)
-        if k == z_plan(s)[0]:
-            g = s // GSUB
+        finished = []
+        if k == "start":
+            pair_start(s)
+        elif k == "end":
+            pair_end(s)
+            finished = [SINGLES + 2 * s, SINGLES + 2 * s + 1]
+        else:
+            z_step(s, k)
+            finished = [s] if k == z_plan(s)[0] else []
+        for f in finished:
+            g = f // GSUB
             done[g] += 1
             if done[g] == GSUB:
                 exchange(g)
@@ -274,10 +340,15 @@
     filtered = jnp.sum(acc, axis=1, keepdims=True) * weight
     out[...] = jnp.sum(sky_v[...].astype(F32) * filtered, axis=0, keepdims=True)
 
-    for s in range(NSUB):
+    for s in range(SINGLES):
         blocks = pl.ds(0, NP - 1)
         pltpu.make_async_copy(vb.at[s, blocks], vb.at[s, blocks], s1_send.at[s]).wait()
         pltpu.make_async_copy(zbuf.at[s], zbuf.at[s], z_send.at[s]).wait()
+    for g in range(PAIRS):
+        blocks = pl.ds(0, NP - 1)
+        pltpu.make_async_copy(pv.at[g], pv.at[g], pair_send.at[g]).wait()
+        pltpu.make_async_copy(xp.at[g, :, blocks], xp.at[g, :, blocks], s1p_send.at[g]).wait()
+        pltpu.make_async_copy(zp.at[g], zp.at[g], zp_send.at[g]).wait()
     for g in range(NG):
         blocks = pl.ds(0, NP - 1)
         pltpu.make_async_copy(ob.at[g, blocks], ob.at[g, blocks], s3_send.at[g]).wait()
@@ -304,7 +375,7 @@
             pltpu.VMEM((levels, multipoles), BF16),
             pltpu.VMEM((NSUB, NP, times, 2 * W), BF16),
             pltpu.VMEM((NSUB, NP, times, 2 * W), BF16),
-            pltpu.VMEM((2, 2 * count, times * NP), BF16),
+            pltpu.VMEM((1 + PAIRS, 2, 2 * count, times * NP), BF16),
             pltpu.VMEM((NSUB, NZ, 4, NP, W), BF16),
             pltpu.VMEM((NSUB, 7, 4, NP, W), BF16),
             pltpu.VMEM((NSUB, 7, 4, NP, W), BF16),
@@ -313,6 +384,10 @@
             pltpu.VMEM((NG, NP, 4 * GSUB, W), BF16),
             dma((4,)), dma((3,)), dma, dma,
             dma((NSUB,)), dma((NSUB,)), dma((NSUB,)), dma((NSUB, LEVELS)), dma((NG,)), dma((NG, NP - 1)),
+            pltpu.VMEM((PAIRS, NP, times, 2 * W), BF16),
+            pltpu.VMEM((PAIRS, 2, NP, times, 2 * W), BF16),
+            pltpu.VMEM((PAIRS, NZ - 1, 4, NP, W), BF16),
+            dma((PAIRS,)), dma((PAIRS,)), dma((PAIRS,)), dma((PAIRS,)), dma((PAIRS,)), dma((PAIRS,)),
         ],
         compiler_params=pltpu.CompilerParams(
             collective_id=0, has_side_effects=True, vmem_limit_bytes=60 * 2**20

time: 41 us -> 38.7 us (0.944)
  Pallas kernels: 39.3 us -> 37.2 us
    pallas_call x1, Pallas kernels: 39.3 us -> 37.2 us  [per_device(): pl.pallas_call(kernel, out_shape=jax.ShapeDtypeStruct((1, multipoles), F3...]
where the time goes in v1:
time: 38.7 us; the launch traced here: 38.5 us
  Pallas kernels  37.2 us (96%)
  local copies, waits for them, and re-layouts  1.3 us (3%)
    pallas_call x1, Pallas kernels, per_device(): pl.pallas_call(kernel, out_shape=jax.ShapeDtypeStruct((1, multipoles), F3...  37.2 us
    unnamed x1, local copies, waits for them, and re-layouts  1.3 us

profile of v1, /device:TPU:2, one launch (start us, length us, event | category | flops | bytes accessed | tf_op | source)
XLA Modules:
  0.0 38.5 jit_solution(2005529505791016868)
XLA Ops:
  0.0 37.2 %shard_map.64 = f32[1,2402]{1,0:T(1,128)} custom-call(f32[2,16,16384]{2,1,0:T(8,128)} %vis.1, s32[1,128]{1,0:T(1,128)} %bitcast.2, s32[1,128]{1,0:T(1,128)} %bitcast.3, bf16[1,64,65536]{2,1,0:T(8,128)(2,1)} %beam.1, f32[1,64]{1,0:T(1,128)} %eigen.1, bf16[1,64,2402]{2,1,0:T(8,128)(2,1)} %sky.1), custom_call_target="tpu_custom_call" | custom-call | tf_op jit(solution)/shard_map/pallas_call | solution.py:364
  37.2 1.3 %copy.8 = f32[1,2402]{1,0:T(1,128)} copy(f32[1,2402]{1,0:T(1,128)} %shard_map.64) | data formatting | bytes 19216

commit v2 on v1

--- a/solution.py
+++ b/solution.py
@@ -180,9 +180,9 @@
         send_blocks(vb.at[s], xs.at[s], s1_send.at[s], s1_recv.at[s])
         return carry
 
-    lax.fori_loop(0, SINGLES, send_single, 0)
-    for g in range(PAIRS):
-        send_blocks(vb.at[kept[g]], xp.at[g, 0], s1p_send.at[g], s1p_recv.at[g])
+    for s in range(SINGLES):
+        send_single(s, 0)
+    send_blocks(vb.at[kept[0]], xp.at[0, 0], s1p_send.at[0], s1p_recv.at[0])
 
     for s in range(SINGLES):
         xs[s, p] = vb[s, p]
@@ -204,6 +204,8 @@
     for g in range(PAIRS):
         pltpu.make_async_copy(pv.at[g], pv.at[g], pair_recv.at[g]).wait()
         send_blocks(pv.at[g], xp.at[g, 1], s1p_send.at[g], s1p_recv.at[g])
+        if g + 1 < PAIRS:
+            send_blocks(vb.at[kept[g + 1]], xp.at[g + 1, 0], s1p_send.at[g + 1], s1p_recv.at[g + 1])
         xp[g, 1, p] = pv[g, p]
     lanes = lax.broadcasted_iota(jnp.int32, (1, modes_total), 1)
     own_mode = jnp.sum(jnp.where(lanes == i, slot_f, 0.0), axis=1, keepdims=True)

time: 38.7 us -> 38.7 us (level)
  no operation moved by 1% of the time
where the time goes in v2:
time: 38.7 us; the launch traced here: 38.5 us
  Pallas kernels  37.2 us (96%)
  local copies, waits for them, and re-layouts  1.3 us (3%)
    pallas_call x1, Pallas kernels, per_device(): pl.pallas_call(kernel, out_shape=jax.ShapeDtypeStruct((1, multipoles), F3...  37.2 us
    unnamed x1, local copies, waits for them, and re-layouts  1.3 us

profile of v2, /device:TPU:2, one launch (start us, length us, event | category | flops | bytes accessed | tf_op | source)
XLA Modules:
  0.0 38.5 jit_solution(2961815429221507443)
XLA Ops:
  0.0 37.2 %shard_map.64 = f32[1,2402]{1,0:T(1,128)} custom-call(f32[2,16,16384]{2,1,0:T(8,128)} %vis.1, s32[1,128]{1,0:T(1,128)} %bitcast.2, s32[1,128]{1,0:T(1,128)} %bitcast.3, bf16[1,64,65536]{2,1,0:T(8,128)(2,1)} %beam.1, f32[1,64]{1,0:T(1,128)} %eigen.1, bf16[1,64,2402]{2,1,0:T(8,128)(2,1)} %sky.1), custom_call_target="tpu_custom_call" | custom-call | tf_op jit(solution)/shard_map/pallas_call | solution.py:366
  37.2 1.3 %copy.8 = f32[1,2402]{1,0:T(1,128)} copy(f32[1,2402]{1,0:T(1,128)} %shard_map.64) | data formatting | bytes 19216
